TPU v7x, 256 devices: a whole 4x4x8 slice. The times are simulated.
256 devices in a mesh: dp: 8 (over z), row: 32 (over y, x, core).
Axes of the slice: x: 4, y: 4, z: 8, core: 2. Of those that a mesh axis runs over, the one named last changes fastest.
Arguments:
- fields: bfloat16 [8, 16, 2048, 2048], P('dp', None, 'row'), may hold values from -6 to 6
- cotangent: bfloat16 [8, 16, 2048, 2048], P('dp', None, 'row'), may hold values from -6 to 6
- spectral: bfloat16 [2, 16, 16, 128, 128], P(None, None, None, 'row'), may hold values from -5 to 5
- local_weight: bfloat16 [16, 16], replicated, may hold values from -1.5 to 1.5
- bias: float32 [16], replicated, may hold values from -3 to 3
Outputs:
- field_grad: bfloat16 [8, 16, 2048, 2048], P('dp', None, 'row')
- spectral_grad: float32 [2, 16, 16, 128, 128], P(None, None, 'dp', 'row')
- local_grad: float32 [16, 16], replicated
- bias_grad: float32 [16], replicated
All inputs are finite; a program needn't handle non-finite values.
Results may differ from a plain program's by a relative error of at most 0.028.
Values may be sent and summed in bfloat16 or wider, within the bound.
A program may use at most 128 MiB of HBM per device.

v0:
```python
import functools
import math

import jax
import jax.numpy as jnp
import ml_dtypes
import numpy as np
from jax import lax
from jax.experimental import pallas as pl
from jax.experimental.pallas import tpu as pltpu
from jax.sharding import Mesh
from jax.sharding import PartitionSpec as P

ROW = ("row_0", "row_1", "row_2")
MESH = pl.DeviceIdType.MESH
F32 = jnp.float32
BF16 = jnp.bfloat16
SIDE = 4
CHIPS = SIDE * SIDE
GROUPS = 4
OFFSETS = (4, 0, 3, 5, 2, 6, 1, 7)
STEP = 512


def angles(freq, pos, count):
    turns = (freq[:, None] % count) * pos[None, :] % count
    return np.float32(2.0 * math.pi / count) * turns.astype(np.float32)


def column_tables(width, modes):
    angle = angles(np.arange(modes), np.arange(width), width)
    both = np.stack([np.cos(angle), -np.sin(angle)], axis=0).astype(ml_dtypes.bfloat16)
    inverse = both.reshape(2 * modes, width)
    return np.ascontiguousarray(inverse.T), inverse


def row_tables(height, modes, owners, scale):
    angle = angles(np.arange(modes) - modes // 2, np.arange(height), height)
    cos = np.cos(angle).astype(ml_dtypes.bfloat16).astype(np.float32) * scale
    sin = np.sin(angle).astype(ml_dtypes.bfloat16).astype(np.float32) * scale
    rows = height // owners
    each = modes // owners

    def split(table):
        table = table.reshape(CHIPS, 2, each, owners, rows)
        return table.transpose(3, 1, 0, 2, 4)

    cos, sin = split(cos), split(sin)
    forward = np.stack(
        [np.stack([cos, sin], axis=-2), np.stack([-sin, cos], axis=-2)], axis=3
    )
    half = forward.transpose(0, 5, 6, 1, 2, 3, 4)
    inverse = np.zeros((owners, 2) + half.shape[1:6] + (2, each), np.float32)
    for pair in range(2):
        inverse[:, pair, :, :, :, :, :, pair, :] = half
    forward = forward.reshape(owners, 2 * modes, 2 * rows)
    inverse = inverse.reshape(owners, 4 * rows, 4 * modes)
    return forward.astype(ml_dtypes.bfloat16), inverse.astype(ml_dtypes.bfloat16)


def dot(a, b):
    return jnp.dot(a, b, preferred_element_type=F32)


def wait_for(ref, sem):
    pltpu.make_async_copy(ref, ref, sem).wait()


def gelu_slope(x):
    k0 = math.sqrt(2.0 / math.pi)
    u = x * (k0 + (k0 * 0.044715) * (x * x))
    t = jnp.tanh(u)
    q = 1.5 * u - k0 * x
    return (1.0 + t) * (0.5 + q * (1.0 - t))


def spread_matrix(lw, transposed):
    i = lax.broadcasted_iota(jnp.int32, (256, 16), 0)
    j = lax.broadcasted_iota(jnp.int32, (256, 16), 1)
    pick = jnp.where(i // 16 == j, 1.0, 0.0).astype(BF16)
    if transposed:
        left = lax.dot_general(pick, lw, (((1,), (1,)), ((), ())), preferred_element_type=F32)
    else:
        left = dot(pick, lw)
    full = lax.dot_general(
        left.astype(BF16), pick, (((1,), (1,)), ((), ())), preferred_element_type=F32
    )
    i = lax.broadcasted_iota(jnp.int32, (256, 256), 0)
    j = lax.broadcasted_iota(jnp.int32, (256, 256), 1)
    return jnp.where(i % 16 == j % 16, full, 0.0).astype(BF16)


def exchange_kernel(
    fields, cot, spec, lw, bias, colf_h, coli_h, rowf_h, rowi_h,
    dy_o, lc_o, sg_o, sums_o,
    fbuf, cbuf, lbuf, gpbuf, lcbuf, wbf, wf, colf, coli, rowf, rowi,
    snd1, sib1, hb1, rcv1, snd2, sib2, hb2, rcv2, ga1, ga2,
    frd, fid, dfr, dfi, gbuf, ybuf, dybuf, bacc, lacc, dwsnd, dwrcv,
    pay, paysib, payrow, paydp,
    ld_f, ld, out_sem,
    ss1, rs1, ss2, rs2, ds1, dr1, ds2, dr2,
    as1, ar1, fs1, fr1, as2, ar2, fs2, fr2, dws, dwr, ps, pr,
):
    z = lax.axis_index("dp")
    y = lax.axis_index("row_0")
    x = lax.axis_index("row_1")
    core = lax.axis_index("row_2")
    other = 1 - core
    chip = y * SIDE + x
    row = chip * 2 + core

    barrier = pltpu.get_barrier_semaphore()

    def peer(k):
        ty = lax.rem(y + k // SIDE, SIDE)
        tx = lax.rem(x + k % SIDE, SIDE)
        return ty, tx

    for k in range(1, CHIPS):
        ty, tx = peer(k)
        pl.semaphore_signal(
            barrier, inc=1, device_id={"row_0": ty, "row_1": tx}, device_id_type=MESH
        )
    pl.semaphore_signal(barrier, inc=1, device_id={"row_2": other}, device_id_type=MESH)
    for k in range(1, 8):
        pl.semaphore_signal(
            barrier, inc=1, device_id={"dp": lax.rem(z + k, 8)}, device_id_type=MESH
        )

    def load(src, dst, sem):
        copy = pltpu.make_async_copy(src, dst, sem)
        copy.start()
        return copy

    l_colf = load(colf_h, colf, ld.at[0])
    l_f = [load(fields.at[pl.ds(0, 4)], fbuf.at[pl.ds(0, 4)], ld_f.at[0])]
    l_rowf = load(rowf_h.at[row], rowf, ld.at[1])
    for g in range(1, GROUPS):
        l_f.append(load(fields.at[pl.ds(4 * g, 4)], fbuf.at[pl.ds(4 * g, 4)], ld_f.at[g]))
    l_w = load(spec, wbf, ld.at[2])
    l_rowi = load(rowi_h.at[row], rowi, ld.at[3])
    l_coli = load(coli_h, coli, ld.at[4])
    l_cot = load(cot, cbuf, ld.at[5])

    def to_sibling(src, dst, ssem, rsem):
        pltpu.make_async_remote_copy(
            src_ref=src, dst_ref=dst, send_sem=ssem, recv_sem=rsem,
            device_id={"row_2": other}, device_id_type=MESH,
        ).start()

    def to_chips(src_of, dst, ssem, rsem):
        def body(k, carry):
            ty, tx = peer(k)
            pltpu.make_async_remote_copy(
                src_ref=src_of(ty * SIDE + tx), dst_ref=dst, send_sem=ssem, recv_sem=rsem,
                device_id={"row_0": ty, "row_1": tx}, device_id_type=MESH,
            ).start()
            return carry

        lax.fori_loop(1, CHIPS, body, 0)

    def row_transform(xb, snd, g):
        for j in range(2):
            cols = []
            for c in range(2):
                at = 128 * j + 64 * c
                cols.append(jnp.concatenate([xb[at : at + 64, :128], xb[at : at + 64, 128:]], axis=0))
            p = dot(rowf[...], jnp.concatenate(cols, axis=1))
            blk = jnp.concatenate(
                [p[:, :128].reshape(32, 8, 128), p[:, 128:].reshape(32, 8, 128)], axis=1
            ).astype(BF16)
            snd[g, :, :, 16 * j : 16 * j + 16, :] = blk.reshape(2, CHIPS, 16, 128)

    def start_sibling(snd, sib, ss, rs, g):
        to_sibling(snd.at[g, other], sib.at[g], ss.at[g], rs.at[g])

    def pass_on(snd, sib, hb, rcv, rs, ds, dr, g):
        wait_for(sib.at[g], rs.at[g])
        hb[g] = (snd[g, core].astype(F32) + sib[g].astype(F32)).astype(BF16)
        to_chips(lambda d: hb.at[g, d], rcv.at[g, chip], ds.at[g], dr.at[g])
        rcv[g, pl.ds(chip, 1)] = hb[g, pl.ds(chip, 1)]

    def arrived(rcv, dr, g):
        wait_for(rcv.at[g, pl.ds(0, CHIPS - 1)], dr.at[g])
        return jnp.sum(rcv[g].astype(F32), axis=0)

    def gather_start(ga, asem, arsem, g):
        to_chips(lambda d: ga.at[g, core, chip], ga.at[g, core, chip], asem.at[g], arsem.at[g])

    def gather_forward(ga, arsem, fs, fr, g):
        wait_for(ga.at[g, core, pl.ds(0, CHIPS - 1)], arsem.at[g])
        to_sibling(ga.at[g, core], ga.at[g, core], fs.at[g], fr.at[g])

    def gather_end(ga, fr, g):
        wait_for(ga.at[g, other], fr.at[g])

    def row_inverse(ga, g):
        parts = [ga[g, :, :, 16 * j : 16 * j + 16, :].reshape(512, 128) for j in range(2)]
        out = dot(rowi[...], jnp.concatenate(parts, axis=1)).astype(BF16)
        rows = []
        for j in range(2):
            for o in range(2):
                block = out[128 * o : 128 * o + 128, 128 * j : 128 * j + 128]
                rows.append(jnp.concatenate([block[:64], block[64:]], axis=1))
        return jnp.concatenate(rows, axis=0)

    l_colf.wait()
    for g in range(GROUPS):
        l_f[g].wait()
        xb = dot(fbuf[4 * g : 4 * g + 4].reshape(256, 2048), colf[...]).astype(BF16)
        if g == 0:
            l_rowf.wait()
        row_transform(xb, snd1, g)
        if g == 0:
            pl.semaphore_wait(barrier, CHIPS + 7)
        start_sibling(snd1, sib1, ss1, rs1, g)
        if g > 0:
            pass_on(snd1, sib1, hb1, rcv1, rs1, ds1, dr1, g - 1)

    i = lax.broadcasted_iota(jnp.int32, (256, 16), 0)
    j = lax.broadcasted_iota(jnp.int32, (256, 16), 1)
    bias_col = jnp.sum(jnp.where(i // 16 == j, bias[...], 0.0), axis=1, keepdims=True)
    mix_fwd = spread_matrix(lw[...], True)

    def local_block(block):
        at = pl.ds(pl.multiple_of(block * 16, 16), 16)
        for w in range(0, 2048, STEP):
            part = dot(mix_fwd, fbuf[:, at, w : w + STEP].reshape(256, STEP)) + bias_col
            lbuf[:, at, w : w + STEP] = part.reshape(16, 16, STEP)

    local_block(0)
    pass_on(snd1, sib1, hb1, rcv1, rs1, ds1, dr1, GROUPS - 1)
    local_block(1)
    l_w.wait()

    def widen(c, carry):
        at = pl.ds(pl.multiple_of(c * 64, 64), 64)
        for part in range(2):
            wf[part, c] = wbf[part, at, :].astype(F32).reshape(8, 8, 128)
        return carry

    lax.fori_loop(0, 16, widen, 0)

    for g in range(GROUPS):
        total = arrived(rcv1, dr1, g)
        for c in range(4):
            real = total[8 * c : 8 * c + 4]
            imag = total[8 * c + 4 : 8 * c + 8]
            frd[4 * g + c] = jnp.concatenate([real, real], axis=0)
            fid[4 * g + c] = jnp.concatenate([imag, imag], axis=0)

    lane = lax.broadcasted_iota(jnp.int32, (8, 128), 1)
    double = jnp.where(lane == 0, 1.0, 2.0).astype(F32)

    def mix(c, carry):
        real, imag = carry
        wr, wi = wf[0, c], wf[1, c]
        fr, fi = frd[c][None], fid[c][None]
        return real + wr * fr - wi * fi, imag + wr * fi + wi * fr

    zero = jnp.zeros((8, 8, 128), F32)
    real, imag = lax.fori_loop(0, 16, mix, (zero, zero))
    gbuf[...] = (jnp.concatenate([real, imag], axis=1) * jnp.concatenate([double, double], axis=0)).astype(BF16)

    def pair_at(p):
        return lax.rem(z + OFFSETS[p], 8)

    for g in range(GROUPS):
        for j in range(2):
            ga1[g, core, chip, 16 * j : 16 * j + 16, :] = gbuf[pair_at(2 * g + j)]
        gather_start(ga1, as1, ar1, g)
    local_block(2)
    local_block(3)
    l_cot.wait()
    l_rowi.wait()
    l_coli.wait()
    gather_forward(ga1, ar1, fs1, fr1, 0)
    dfr[...] = jnp.zeros_like(dfr)
    dfi[...] = jnp.zeros_like(dfi)

    def gradient_arrived(g):
        total = arrived(rcv2, dr2, g)
        for j in range(2):
            q = pair_at(2 * g + j)
            a, b = total[16 * j : 16 * j + 8], total[16 * j + 8 : 16 * j + 16]
            gr = jnp.concatenate([a[:4], b[:4]], axis=0) * double
            gi = jnp.concatenate([a[4:], b[4:]], axis=0) * double
            slot = 2 * g + j
            wr = wf[0, :, pl.ds(q, 1)].reshape(16, 8, 128)
            wi = wf[1, :, pl.ds(q, 1)].reshape(16, 8, 128)
            fr, fi = frd[...], fid[...]
            dfr[...] += wr * gr[None] + wi * gi[None]
            dfi[...] += wr * gi[None] - wi * gr[None]
            term = jnp.concatenate(
                [
                    (gr[None] * fr + gi[None] * fi).reshape(128, 128),
                    (gi[None] * fr - gr[None] * fi).reshape(128, 128),
                ],
                axis=0,
            ).astype(BF16)
            if OFFSETS[slot] == 0:
                dwrcv[pl.ds(z, 1)] = term[None]
            else:
                dwsnd[slot] = term
                pltpu.make_async_remote_copy(
                    src_ref=dwsnd.at[slot], dst_ref=dwrcv.at[z], send_sem=dws.at[slot],
                    recv_sem=dwr, device_id={"dp": q}, device_id_type=MESH,
                ).start()

    for g in range(GROUPS):
        gather_end(ga1, fr1, g)
        ybuf[...] = row_inverse(ga1, g)
        pairs = [pair_at(2 * g), pair_at(2 * g + 1)]

        def chunk(w, acc):
            at = pl.ds(pl.multiple_of(w * STEP, STEP), STEP)
            out = dot(ybuf[...], coli[:, at])
            grads = []
            for j in range(2):
                o = pl.ds(2 * pairs[j], 2)
                pre = out[128 * j : 128 * j + 128] + lbuf[o, :, at].reshape(128, STEP)
                grad = cbuf[o, :, at].reshape(128, STEP).astype(F32) * gelu_slope(pre)
                grad = grad.astype(BF16)
                gpbuf[o, :, at] = grad.reshape(2, 64, STEP)
                grads.append(grad)
            return acc + dot(jnp.concatenate(grads, axis=0), colf[at, :])

        acc = lax.fori_loop(0, 2, chunk, jnp.zeros((256, 256), F32))
        if g > 0:
            pass_on(snd2, sib2, hb2, rcv2, rs2, ds2, dr2, g - 1)
        if g + 1 < GROUPS:
            gather_forward(ga1, ar1, fs1, fr1, g + 1)
        acc = lax.fori_loop(2, 4, chunk, acc)
        for j in range(2):
            for o in range(2):
                at = 128 * j + 64 * o
                bacc[2 * pairs[j] + o] = jnp.sum(acc[at : at + 64, :128].reshape(8, 8, 128), axis=0)
        row_transform(acc.astype(BF16), snd2, g)
        start_sibling(snd2, sib2, ss2, rs2, g)
        if g > 1:
            gradient_arrived(g - 2)

    nt = (((1,), (1,)), ((), ()))

    def outer_block(block):
        at = pl.ds(block * 16, 16)
        return lax.dot_general(
            fbuf[:, at, :].reshape(256, 2048), gpbuf[:, at, :].reshape(256, 2048), nt,
            preferred_element_type=F32,
        )

    mix_bwd = spread_matrix(lw[...], False)
    lc_copies = []

    def back_block(block):
        at = pl.ds(block * 16, 16)
        for w in range(0, 2048, STEP):
            part = dot(mix_bwd, gpbuf[:, at, w : w + STEP].reshape(256, STEP))
            lcbuf[:, at, w : w + STEP] = part.astype(BF16).reshape(16, 16, STEP)
        copy = pltpu.make_async_copy(lcbuf.at[:, at, :], lc_o.at[:, at, :], out_sem.at[block])
        copy.start()
        lc_copies.append(copy)

    lacc[...] = outer_block(0)
    pass_on(snd2, sib2, hb2, rcv2, rs2, ds2, dr2, GROUPS - 1)
    lacc[...] += outer_block(1)
    gradient_arrived(GROUPS - 2)
    lacc[...] += outer_block(2)
    lacc[...] += outer_block(3)

    i = lax.broadcasted_iota(jnp.int32, (256, 256), 0)
    j = lax.broadcasted_iota(jnp.int32, (256, 256), 1)
    kept = jnp.where(i % 16 == j % 16, lacc[...], 0.0)
    kept = jnp.sum(kept.reshape(16, 16, 256), axis=1)
    i = lax.broadcasted_iota(jnp.int32, (256, 128), 0)
    j = lax.broadcasted_iota(jnp.int32, (256, 128), 1)
    pick = jnp.where(i // 16 == j, 1.0, 0.0).astype(F32)
    local = jnp.dot(kept, pick, preferred_element_type=F32, precision=lax.Precision.HIGHEST)
    first = jnp.sum(jnp.sum(bacc[...], axis=1)[:, :1], axis=1, keepdims=True)
    lane16 = lax.broadcasted_iota(jnp.int32, (16, 128), 1)
    pay[0] = jnp.where(lane16 == 16, first, local)
    to_sibling(pay.at[0], paysib, ps.at[0], pr.at[0])

    gradient_arrived(GROUPS - 1)

    for g in range(GROUPS):
        for j in range(2):
            c = 4 * g + 2 * j
            parts = []
            for ref in (dfr, dfi):
                for k in range(2):
                    both = ref[c + k]
                    parts.append(both[:4] + both[4:])
            ga2[g, core, chip, 16 * j : 16 * j + 16, :] = jnp.concatenate(parts, axis=0).astype(BF16)
        gather_start(ga2, as2, ar2, g)

    back_block(0)
    wait_for(paysib, pr.at[0])
    pay[1] = pay[0] + paysib[...]
    to_chips(lambda d: pay.at[1], payrow.at[chip], ps.at[1], pr.at[1])
    payrow[pl.ds(chip, 1)] = pay[pl.ds(1, 1)]
    back_block(1)
    back_block(2)
    back_block(3)
    wait_for(payrow.at[pl.ds(0, CHIPS - 1)], pr.at[1])
    pay[2] = jnp.sum(payrow[...], axis=0)
    for k in range(1, 8):
        pltpu.make_async_remote_copy(
            src_ref=pay.at[2], dst_ref=paydp.at[z], send_sem=ps.at[2], recv_sem=pr.at[2],
            device_id={"dp": lax.rem(z + k, 8)}, device_id_type=MESH,
        ).start()
    paydp[pl.ds(z, 1)] = pay[pl.ds(2, 1)]

    dy_copies = []
    gather_forward(ga2, ar2, fs2, fr2, 0)
    for g in range(GROUPS):
        if g + 1 < GROUPS:
            gather_forward(ga2, ar2, fs2, fr2, g + 1)
        gather_end(ga2, fr2, g)
        dybuf[4 * g : 4 * g + 4] = row_inverse(ga2, g).reshape(4, 64, 256)
        copy = pltpu.make_async_copy(
            dybuf.at[pl.ds(4 * g, 4)], dy_o.at[pl.ds(4 * g, 4)], out_sem.at[4 + g]
        )
        copy.start()
        dy_copies.append(copy)

    wait_for(dwrcv.at[pl.ds(0, 7)], dwr)
    total = dwrcv[0].astype(F32)
    for k in range(1, 8):
        total = total + dwrcv[k].astype(F32)
    sg_o[...] = total.reshape(32, 8, 128)

    wait_for(paydp.at[pl.ds(0, 7)], pr.at[2])
    scale = 1.0 / math.sqrt(8 * 2048 * 2048)
    sums_o[...] = scale * jnp.sum(paydp[...], axis=0)

    for g in range(GROUPS):
        wait_for(snd1.at[g, 0], ss1.at[g])
        wait_for(hb1.at[g, pl.ds(0, CHIPS - 1)], ds1.at[g])
        wait_for(snd2.at[g, 0], ss2.at[g])
        wait_for(hb2.at[g, pl.ds(0, CHIPS - 1)], ds2.at[g])
        wait_for(ga1.at[g, core, pl.ds(0, CHIPS - 1)], as1.at[g])
        wait_for(ga1.at[g, core], fs1.at[g])
        wait_for(ga2.at[g, core, pl.ds(0, CHIPS - 1)], as2.at[g])
        wait_for(ga2.at[g, core], fs2.at[g])
    for slot in range(8):
        if OFFSETS[slot] != 0:
            wait_for(dwsnd.at[slot], dws.at[slot])
    wait_for(pay.at[0], ps.at[0])
    wait_for(payrow.at[pl.ds(0, CHIPS - 1)], ps.at[1])
    wait_for(paydp.at[pl.ds(0, 7)], ps.at[2])
    for copy in lc_copies + dy_copies:
        copy.wait()


def combine_kernel(dy, lc, coli, out):
    chans = dy.shape[0]
    spectral = dot(dy[...].reshape(chans * 64, 256), coli[...])
    out[...] = (spectral + lc[...].reshape(chans * 64, 2048).astype(F32)).astype(BF16).reshape(out.shape)


def on_device(fields, cotangent, spectral, local_weight, bias):
    chans, rows, width = fields.shape[1:]
    modes = spectral.shape[4]
    height = rows * 2 * CHIPS
    scale = 1.0 / math.sqrt(height * width)
    colf, coli = column_tables(width, modes)
    rowf, rowi = row_tables(height, modes, 2 * CHIPS, scale)
    colf, coli, rowf, rowi = (jnp.asarray(t) for t in (colf, coli, rowf, rowi))
    anywhere = pl.BlockSpec(memory_space=pl.ANY)
    vmem = pl.BlockSpec(memory_space=pltpu.VMEM)
    dma = pltpu.SemaphoreType.DMA
    big = (16, 64, 2048)
    reduce_bufs = [
        pltpu.VMEM((GROUPS, 2, CHIPS, 32, 128), BF16),
        pltpu.VMEM((GROUPS, CHIPS, 32, 128), BF16),
        pltpu.VMEM((GROUPS, CHIPS, 32, 128), BF16),
        pltpu.VMEM((GROUPS, CHIPS, 32, 128), BF16),
    ]
    gather_buf = pltpu.VMEM((GROUPS, 2, CHIPS, 32, 128), BF16)
    tile16 = pltpu.VMEM((16, 8, 128), F32)
    scratch = [
        pltpu.VMEM(big, BF16),
        pltpu.VMEM(big, BF16),
        pltpu.VMEM(big, F32),
        pltpu.VMEM(big, BF16),
        pltpu.VMEM(big, BF16),
        pltpu.VMEM((2, 1024, 128), BF16),
        pltpu.VMEM((2, 16, 8, 8, 128), F32),
        pltpu.VMEM(colf.shape, BF16),
        pltpu.VMEM(coli.shape, BF16),
        pltpu.VMEM(rowf.shape[1:], BF16),
        pltpu.VMEM(rowi.shape[1:], BF16),
        *reduce_bufs,
        *reduce_bufs,
        gather_buf,
        gather_buf,
        tile16,
        tile16,
        tile16,
        tile16,
        pltpu.VMEM((8, 16, 128), BF16),
        pltpu.VMEM((256, 256), BF16),
        pltpu.VMEM((16, 64, 256), BF16),
        tile16,
        pltpu.VMEM((256, 256), F32),
        pltpu.VMEM((8, 256, 128), BF16),
        pltpu.VMEM((8, 256, 128), BF16),
        pltpu.VMEM((3, 16, 128), F32),
        pltpu.VMEM((16, 128), F32),
        pltpu.VMEM((CHIPS, 16, 128), F32),
        pltpu.VMEM((8, 16, 128), F32),
        dma((GROUPS,)),
        dma((6,)),
        dma((8,)),
        *[dma((GROUPS,)) for _ in range(16)],
        dma((8,)),
        dma(()),
        dma((3,)),
        dma((3,)),
    ]
    dy, lc, sg, sums = pl.pallas_call(
        exchange_kernel,
        out_shape=(
            jax.ShapeDtypeStruct((16, 64, 256), BF16),
            jax.ShapeDtypeStruct(big, BF16),
            jax.ShapeDtypeStruct((32, 8, 128), F32),
            jax.ShapeDtypeStruct((16, 128), F32),
        ),
        in_specs=[anywhere, anywhere, anywhere, vmem, vmem, anywhere, anywhere, anywhere, anywhere],
        out_specs=(anywhere, anywhere, vmem, vmem),
        scratch_shapes=scratch,
        compiler_params=pltpu.CompilerParams(
            collective_id=0, has_side_effects=True, vmem_limit_bytes=58 * 2**20
        ),
        cost_estimate=pl.CostEstimate(flops=8 * 10**9, bytes_accessed=16 * 2**20, transcendentals=2**21),
        name="layer_exchange",
    )(
        fields[0], cotangent[0], spectral.reshape(2, 1024, 128), local_weight, bias[None, :],
        colf, coli, rowf, rowi,
    )
    step = 2
    grad = pl.pallas_call(
        combine_kernel,
        grid=(chans // step,),
        out_shape=jax.ShapeDtypeStruct((1,) + big, BF16),
        in_specs=[
            pl.BlockSpec((step, 64, 256), lambda i: (i, 0, 0)),
            pl.BlockSpec((step, 64, 2048), lambda i: (i, 0, 0)),
            pl.BlockSpec((256, 2048), lambda i: (0, 0)),
        ],
        out_specs=pl.BlockSpec((1, step, 64, 2048), lambda i: (0, i, 0, 0)),
        compiler_params=pltpu.CompilerParams(vmem_limit_bytes=32 * 2**20),
        cost_estimate=pl.CostEstimate(flops=10**9, bytes_accessed=9 * 2**20, transcendentals=0),
        name="map_gradient",
    )(dy, lc, coli)
    return grad, sg.reshape(2, 16, 2, 4, 128), sums[:, :16], sums[:, 16]


def solution(mesh):
    finer = Mesh(mesh.devices.reshape(mesh.shape["dp"], 4, 4, 2), ("dp", "row_0", "row_1", "row_2"))
    placed = (
        P("dp", None, ROW, None),
        P("dp", None, ROW, None),
        P(None, None, None, ROW, None),
        P(),
        P(),
    )
    return jax.shard_map(
        on_device,
        mesh=finer,
        in_specs=placed,
        out_specs=(P("dp", None, ROW, None), P(None, None, "dp", ROW, None), P(), P()),
        check_vma=False,
    )
```

profile of v0, /device:TPU:1, one launch (start us, length us, event | category | flops | bytes accessed | tf_op | source)
XLA Modules:
  0.0 74.4 jit_solution(3402732549668771850)
XLA Ops:
  0.6 0.0 copy-start.1
  0.6 63.8 %layer_exchange.1 = (bf16[16,64,256]{2,1,0:T(8,128)(2,1)}, bf16[16,64,2048]{2,1,0:T(8,128)(2,1)}, f32[32,8,128]{2,1,0:T(8,128)}, f32[16,128]{1,0:T(8,128)}) custom-call(bf16[16,64,2048]{2,1,0:T(8,128)(2,1)} %bitcast.8, bf16[16,64,2048]{2,1,0:T(8,128)(2,1)} %bitcast.9, bf16[2,1024,128]{2,1,0:T(8,128)(2,1)} %bitcast.10, bf16[16,16]{1,0:T(8,128)(2,1)} %lw.1, ...), custom_call_target="tpu_custom_call" | custom-call | flops 8000000000 | bytes 16777216 | tf_op jit(solution)/shard_map/layer_exchange/pallas_call | solution.py:522
  64.4 0.0 copy-done.1
  64.5 0.0 copy-start
  64.5 2.2 %copy-done = bf16[16,64,2048]{2,1,0:T(8,128)(2,1)S(1)} copy-done((bf16[16,64,2048]{2,1,0:T(8,128)(2,1)S(1)}, bf16[16,64,2048]{2,1,0:T(8,128)(2,1)}, u32[]{:S(2)}) %copy-start) | copy-done | bytes 4194328
  66.6 0.0 copy-start.2
  66.7 1.0 %copy-done.2 = bf16[16,64,256]{2,1,0:T(8,128)(2,1)S(1)} copy-done((bf16[16,64,256]{2,1,0:T(8,128)(2,1)S(1)}, bf16[16,64,256]{2,1,0:T(8,128)(2,1)}, u32[]{:S(2)}) %copy-start.2) | copy-done | bytes 524312
  67.7 0.0 copy-start.4
  67.7 0.0 copy-start.3
  67.7 4.8 %map_gradient.1 = bf16[1,16,64,2048]{3,2,1,0:T(8,128)(2,1)} custom-call(bf16[16,64,256]{2,1,0:T(8,128)(2,1)S(1)} %copy-done.2, bf16[16,64,2048]{2,1,0:T(8,128)(2,1)S(1)} %copy-done, bf16[256,2048]{1,0:T(8,128)(2,1)S(1)} %copy-done.1), custom_call_target="tpu_custom_call" | custom-call | flops 1000000000 | bytes 9437184 | tf_op jit(solution)/shard_map/map_gradient/pallas_call | solution.py:543
  72.4 0.0 copy-done.4
  72.5 0.7 slice_reduce_fusion
  73.1 0.0 copy-done.3
  73.1 0.7 copy.15
  73.8 0.6 copy.16
Async XLA Ops:
  0.6 63.8 %copy-start.1 = (bf16[256,2048]{1,0:T(8,128)(2,1)S(1)}, bf16[256,2048]{1,0:T(8,128)(2,1)}, u32[]{:S(2)}) copy-start(bf16[256,2048]{1,0:T(8,128)(2,1)} %constant.9.clone.coli_h.coli) | copy-start | bytes 3145732
  64.5 2.2 %copy-start = (bf16[16,64,2048]{2,1,0:T(8,128)(2,1)S(1)}, bf16[16,64,2048]{2,1,0:T(8,128)(2,1)}, u32[]{:S(2)}) copy-start(bf16[16,64,2048]{2,1,0:T(8,128)(2,1)} %get-tuple-element.9.lc) | copy-start | bytes 12582916
  66.6 1.0 %copy-start.2 = (bf16[16,64,256]{2,1,0:T(8,128)(2,1)S(1)}, bf16[16,64,256]{2,1,0:T(8,128)(2,1)}, u32[]{:S(2)}) copy-start(bf16[16,64,256]{2,1,0:T(8,128)(2,1)} %get-tuple-element.8.dy) | copy-start | bytes 1572868
  67.7 4.8 %copy-start.4 = (f32[16,128]{1,0:T(8,128)S(1)}, f32[16,128]{1,0:T(8,128)}, u32[]{:S(2)}) copy-start(f32[16,128]{1,0:T(8,128)} %get-tuple-element.11) | copy-start | bytes 24580
  67.7 5.5 %copy-start.3 = (f32[32,8,128]{2,1,0:T(8,128)S(1)}, f32[32,8,128]{2,1,0:T(8,128)}, u32[]{:S(2)}) copy-start(f32[32,8,128]{2,1,0:T(8,128)} %get-tuple-element.10) | copy-start | bytes 393220
where the time goes:
time: 74.6 us; the launch traced here: 74.4 us
  Pallas kernels  68.6 us (92%)
  local copies, waits for them, and re-layouts  5.18 us (7%)
    pallas_call x1, Pallas kernels, on_device(): pl.pallas_call(exchange_kernel, out_shape=(jax.ShapeDtypeStruct((16, 64,...  63.8 us
    pallas_call x1, Pallas kernels, on_device(): pl.pallas_call(combine_kernel, grid=(chans // step,), out_shape=jax.Shape...  4.75 us
    unnamed x12, local copies, waits for them, and re-layouts  4.49 us

commit v1 on v0

--- a/solution.py
+++ b/solution.py
@@ -20,6 +20,10 @@
 GROUPS = 4
 OFFSETS = (4, 0, 3, 5, 2, 6, 1, 7)
 STEP = 512
+PEERS = sorted(
+    ((dy, dx) for dy in range(SIDE) for dx in range(SIDE) if dy or dx),
+    key=lambda p: -(min(p[0], SIDE - p[0]) + min(p[1], SIDE - p[1])),
+)
 
 
 def angles(freq, pos, count):
@@ -68,10 +72,12 @@
 
 def gelu_slope(x):
     k0 = math.sqrt(2.0 / math.pi)
-    u = x * (k0 + (k0 * 0.044715) * (x * x))
-    t = jnp.tanh(u)
-    q = 1.5 * u - k0 * x
-    return (1.0 + t) * (0.5 + q * (1.0 - t))
+    one = BF16
+    x = x.astype(BF16)
+    a = one(k0 * 0.044715) * (x * x)
+    t = jnp.tanh(x * (a + one(k0)))
+    q = x * (one(1.5) * a + one(0.5 * k0))
+    return (one(1.0) + t) * (one(0.5) + q * (one(1.0) - t))
 
 
 def spread_matrix(lw, transposed):
@@ -91,13 +97,13 @@
 
 
 def exchange_kernel(
-    fields, cot, spec, lw, bias, colf_h, coli_h, rowf_h, rowi_h,
-    dy_o, lc_o, sg_o, sums_o,
-    fbuf, cbuf, lbuf, gpbuf, lcbuf, wbf, wf, colf, coli, rowf, rowi,
+    fields, cot, spec, lw_h, bias_h, colf_h, coli_h, rowf_h, rowi_h,
+    fg_o, sg_o, sums_o,
+    lw, bias, fbuf, cbuf, lbuf, gpbuf, wbf, wf, colf, coli, rowf, rowi,
     snd1, sib1, hb1, rcv1, snd2, sib2, hb2, rcv2, ga1, ga2,
-    frd, fid, dfr, dfi, gbuf, ybuf, dybuf, bacc, lacc, dwsnd, dwrcv,
+    frd, fid, dfr, dfi, gbuf, ybuf, bacc, lacc, dwsnd, dwrcv,
     pay, paysib, payrow, paydp,
-    ld_f, ld, out_sem,
+    ld_f, ld,
     ss1, rs1, ss2, rs2, ds1, dr1, ds2, dr2,
     as1, ar1, fs1, fr1, as2, ar2, fs2, fr2, dws, dwr, ps, pr,
 ):
@@ -111,13 +117,11 @@
 
     barrier = pltpu.get_barrier_semaphore()
 
-    def peer(k):
-        ty = lax.rem(y + k // SIDE, SIDE)
-        tx = lax.rem(x + k % SIDE, SIDE)
-        return ty, tx
-
-    for k in range(1, CHIPS):
-        ty, tx = peer(k)
+    rows_y = [lax.rem(y + d, SIDE) for d in range(SIDE)]
+    rows_x = [lax.rem(x + d, SIDE) for d in range(SIDE)]
+    peers = [(rows_y[dy], rows_x[dx]) for dy, dx in PEERS]
+
+    for ty, tx in peers:
         pl.semaphore_signal(
             barrier, inc=1, device_id={"row_0": ty, "row_1": tx}, device_id_type=MESH
         )
@@ -138,6 +142,8 @@
     for g in range(1, GROUPS):
         l_f.append(load(fields.at[pl.ds(4 * g, 4)], fbuf.at[pl.ds(4 * g, 4)], ld_f.at[g]))
     l_w = load(spec, wbf, ld.at[2])
+    l_lw = load(lw_h, lw, ld.at[6])
+    l_bias = load(bias_h, bias, ld.at[7])
     l_rowi = load(rowi_h.at[row], rowi, ld.at[3])
     l_coli = load(coli_h, coli, ld.at[4])
     l_cot = load(cot, cbuf, ld.at[5])
@@ -149,15 +155,11 @@
         ).start()
 
     def to_chips(src_of, dst, ssem, rsem):
-        def body(k, carry):
-            ty, tx = peer(k)
+        for ty, tx in peers:
             pltpu.make_async_remote_copy(
                 src_ref=src_of(ty * SIDE + tx), dst_ref=dst, send_sem=ssem, recv_sem=rsem,
                 device_id={"row_0": ty, "row_1": tx}, device_id_type=MESH,
             ).start()
-            return carry
-
-        lax.fori_loop(1, CHIPS, body, 0)
 
     def row_transform(xb, snd, g):
         for j in range(2):
@@ -211,12 +213,16 @@
         if g == 0:
             l_rowf.wait()
         row_transform(xb, snd1, g)
-        if g == 0:
+        if g == GROUPS - 2:
             pl.semaphore_wait(barrier, CHIPS + 7)
-        start_sibling(snd1, sib1, ss1, rs1, g)
-        if g > 0:
-            pass_on(snd1, sib1, hb1, rcv1, rs1, ds1, dr1, g - 1)
-
+            for early in range(GROUPS - 1):
+                start_sibling(snd1, sib1, ss1, rs1, early)
+    start_sibling(snd1, sib1, ss1, rs1, GROUPS - 1)
+    for g in range(GROUPS):
+        pass_on(snd1, sib1, hb1, rcv1, rs1, ds1, dr1, g)
+
+    l_lw.wait()
+    l_bias.wait()
     i = lax.broadcasted_iota(jnp.int32, (256, 16), 0)
     j = lax.broadcasted_iota(jnp.int32, (256, 16), 1)
     bias_col = jnp.sum(jnp.where(i // 16 == j, bias[...], 0.0), axis=1, keepdims=True)
@@ -229,7 +235,6 @@
             lbuf[:, at, w : w + STEP] = part.reshape(16, 16, STEP)
 
     local_block(0)
-    pass_on(snd1, sib1, hb1, rcv1, rs1, ds1, dr1, GROUPS - 1)
     local_block(1)
     l_w.wait()
 
@@ -313,32 +318,29 @@
         pairs = [pair_at(2 * g), pair_at(2 * g + 1)]
 
         def chunk(w, acc):
-            at = pl.ds(pl.multiple_of(w * STEP, STEP), STEP)
+            at = pl.ds(w * STEP, STEP)
             out = dot(ybuf[...], coli[:, at])
             grads = []
             for j in range(2):
                 o = pl.ds(2 * pairs[j], 2)
                 pre = out[128 * j : 128 * j + 128] + lbuf[o, :, at].reshape(128, STEP)
-                grad = cbuf[o, :, at].reshape(128, STEP).astype(F32) * gelu_slope(pre)
-                grad = grad.astype(BF16)
+                grad = cbuf[o, :, at].reshape(128, STEP) * gelu_slope(pre)
                 gpbuf[o, :, at] = grad.reshape(2, 64, STEP)
                 grads.append(grad)
             return acc + dot(jnp.concatenate(grads, axis=0), colf[at, :])
 
-        acc = lax.fori_loop(0, 2, chunk, jnp.zeros((256, 256), F32))
+        acc = chunk(1, chunk(0, jnp.zeros((256, 256), F32)))
         if g > 0:
             pass_on(snd2, sib2, hb2, rcv2, rs2, ds2, dr2, g - 1)
         if g + 1 < GROUPS:
             gather_forward(ga1, ar1, fs1, fr1, g + 1)
-        acc = lax.fori_loop(2, 4, chunk, acc)
+        acc = chunk(3, chunk(2, acc))
         for j in range(2):
             for o in range(2):
                 at = 128 * j + 64 * o
                 bacc[2 * pairs[j] + o] = jnp.sum(acc[at : at + 64, :128].reshape(8, 8, 128), axis=0)
         row_transform(acc.astype(BF16), snd2, g)
         start_sibling(snd2, sib2, ss2, rs2, g)
-        if g > 1:
-            gradient_arrived(g - 2)
 
     nt = (((1,), (1,)), ((), ()))
 
@@ -350,21 +352,18 @@
         )
 
     mix_bwd = spread_matrix(lw[...], False)
-    lc_copies = []
 
     def back_block(block):
         at = pl.ds(block * 16, 16)
         for w in range(0, 2048, STEP):
             part = dot(mix_bwd, gpbuf[:, at, w : w + STEP].reshape(256, STEP))
-            lcbuf[:, at, w : w + STEP] = part.astype(BF16).reshape(16, 16, STEP)
-        copy = pltpu.make_async_copy(lcbuf.at[:, at, :], lc_o.at[:, at, :], out_sem.at[block])
-        copy.start()
-        lc_copies.append(copy)
+            fg_o[:, at, w : w + STEP] = part.astype(BF16).reshape(16, 16, STEP)
 
     lacc[...] = outer_block(0)
     pass_on(snd2, sib2, hb2, rcv2, rs2, ds2, dr2, GROUPS - 1)
+    gradient_arrived(0)
     lacc[...] += outer_block(1)
-    gradient_arrived(GROUPS - 2)
+    gradient_arrived(1)
     lacc[...] += outer_block(2)
     lacc[...] += outer_block(3)
 
@@ -380,6 +379,15 @@
     lane16 = lax.broadcasted_iota(jnp.int32, (16, 128), 1)
     pay[0] = jnp.where(lane16 == 16, first, local)
     to_sibling(pay.at[0], paysib, ps.at[0], pr.at[0])
+    back_block(0)
+    gradient_arrived(2)
+    back_block(1)
+    wait_for(paysib, pr.at[0])
+    pay[1] = pay[0] + paysib[...]
+    to_chips(lambda d: pay.at[1], payrow.at[chip], ps.at[1], pr.at[1])
+    payrow[pl.ds(chip, 1)] = pay[pl.ds(1, 1)]
+    back_block(2)
+    back_block(3)
 
     gradient_arrived(GROUPS - 1)
 
@@ -394,14 +402,6 @@
             ga2[g, core, chip, 16 * j : 16 * j + 16, :] = jnp.concatenate(parts, axis=0).astype(BF16)
         gather_start(ga2, as2, ar2, g)
 
-    back_block(0)
-    wait_for(paysib, pr.at[0])
-    pay[1] = pay[0] + paysib[...]
-    to_chips(lambda d: pay.at[1], payrow.at[chip], ps.at[1], pr.at[1])
-    payrow[pl.ds(chip, 1)] = pay[pl.ds(1, 1)]
-    back_block(1)
-    back_block(2)
-    back_block(3)
     wait_for(payrow.at[pl.ds(0, CHIPS - 1)], pr.at[1])
     pay[2] = jnp.sum(payrow[...], axis=0)
     for k in range(1, 8):
@@ -411,18 +411,18 @@
         ).start()
     paydp[pl.ds(z, 1)] = pay[pl.ds(2, 1)]
 
-    dy_copies = []
     gather_forward(ga2, ar2, fs2, fr2, 0)
     for g in range(GROUPS):
         if g + 1 < GROUPS:
             gather_forward(ga2, ar2, fs2, fr2, g + 1)
         gather_end(ga2, fr2, g)
-        dybuf[4 * g : 4 * g + 4] = row_inverse(ga2, g).reshape(4, 64, 256)
-        copy = pltpu.make_async_copy(
-            dybuf.at[pl.ds(4 * g, 4)], dy_o.at[pl.ds(4 * g, 4)], out_sem.at[4 + g]
-        )
-        copy.start()
-        dy_copies.append(copy)
+        ybuf[...] = row_inverse(ga2, g)
+        for w in range(0, 2048, STEP):
+            spectral = dot(ybuf[...], coli[:, w : w + STEP])
+            local_part = fg_o[4 * g : 4 * g + 4, :, w : w + STEP].reshape(256, STEP).astype(F32)
+            fg_o[4 * g : 4 * g + 4, :, w : w + STEP] = (
+                (spectral + local_part).astype(BF16).reshape(4, 64, STEP)
+            )
 
     wait_for(dwrcv.at[pl.ds(0, 7)], dwr)
     total = dwrcv[0].astype(F32)
@@ -449,14 +449,17 @@
     wait_for(pay.at[0], ps.at[0])
     wait_for(payrow.at[pl.ds(0, CHIPS - 1)], ps.at[1])
     wait_for(paydp.at[pl.ds(0, 7)], ps.at[2])
-    for copy in lc_copies + dy_copies:
-        copy.wait()
-
-
-def combine_kernel(dy, lc, coli, out):
-    chans = dy.shape[0]
-    spectral = dot(dy[...].reshape(chans * 64, 256), coli[...])
-    out[...] = (spectral + lc[...].reshape(chans * 64, 2048).astype(F32)).astype(BF16).reshape(out.shape)
+
+
+def write_kernel(fg, sg, sums, fg_o, sg_o, lg_o, bg_o, sem):
+    copy = pltpu.make_async_copy(fg, fg_o.at[0], sem)
+    copy.start()
+    sg_o[...] = sg[...]
+    lg_o[...] = sums[:, :16]
+    i = lax.broadcasted_iota(jnp.int32, (16, 16), 0)
+    j = lax.broadcasted_iota(jnp.int32, (16, 16), 1)
+    bg_o[...] = jnp.sum(jnp.where(i == j, sums[:, 16:17], 0.0), axis=0, keepdims=True)
+    copy.wait()
 
 
 def on_device(fields, cotangent, spectral, local_weight, bias):
@@ -480,10 +483,11 @@
     gather_buf = pltpu.VMEM((GROUPS, 2, CHIPS, 32, 128), BF16)
     tile16 = pltpu.VMEM((16, 8, 128), F32)
     scratch = [
+        pltpu.VMEM((16, 16), BF16),
+        pltpu.VMEM((1, 16), F32),
         pltpu.VMEM(big, BF16),
         pltpu.VMEM(big, BF16),
         pltpu.VMEM(big, F32),
-        pltpu.VMEM(big, BF16),
         pltpu.VMEM(big, BF16),
         pltpu.VMEM((2, 1024, 128), BF16),
         pltpu.VMEM((2, 16, 8, 8, 128), F32),
@@ -501,7 +505,6 @@
         tile16,
         pltpu.VMEM((8, 16, 128), BF16),
         pltpu.VMEM((256, 256), BF16),
-        pltpu.VMEM((16, 64, 256), BF16),
         tile16,
         pltpu.VMEM((256, 256), F32),
         pltpu.VMEM((8, 256, 128), BF16),
@@ -511,7 +514,6 @@
         pltpu.VMEM((CHIPS, 16, 128), F32),
         pltpu.VMEM((8, 16, 128), F32),
         dma((GROUPS,)),
-        dma((6,)),
         dma((8,)),
         *[dma((GROUPS,)) for _ in range(16)],
         dma((8,)),
@@ -519,19 +521,18 @@
         dma((3,)),
         dma((3,)),
     ]
-    dy, lc, sg, sums = pl.pallas_call(
+    fg, sg, sums = pl.pallas_call(
         exchange_kernel,
         out_shape=(
-            jax.ShapeDtypeStruct((16, 64, 256), BF16),
-            jax.ShapeDtypeStruct(big, BF16),
-            jax.ShapeDtypeStruct((32, 8, 128), F32),
-            jax.ShapeDtypeStruct((16, 128), F32),
+            pltpu.VMEM(big, BF16),
+            pltpu.VMEM((32, 8, 128), F32),
+            pltpu.VMEM((16, 128), F32),
         ),
-        in_specs=[anywhere, anywhere, anywhere, vmem, vmem, anywhere, anywhere, anywhere, anywhere],
-        out_specs=(anywhere, anywhere, vmem, vmem),
+        in_specs=[anywhere] * 9,
+        out_specs=(vmem, vmem, vmem),
         scratch_shapes=scratch,
         compiler_params=pltpu.CompilerParams(
-            collective_id=0, has_side_effects=True, vmem_limit_bytes=58 * 2**20
+            collective_id=0, has_side_effects=True, vmem_limit_bytes=117 * 2**19
         ),
         cost_estimate=pl.CostEstimate(flops=8 * 10**9, bytes_accessed=16 * 2**20, transcendentals=2**21),
         name="layer_exchange",
@@ -539,22 +540,22 @@
         fields[0], cotangent[0], spectral.reshape(2, 1024, 128), local_weight, bias[None, :],
         colf, coli, rowf, rowi,
     )
-    step = 2
-    grad = pl.pallas_call(
-        combine_kernel,
-        grid=(chans // step,),
-        out_shape=jax.ShapeDtypeStruct((1,) + big, BF16),
-        in_specs=[
-            pl.BlockSpec((step, 64, 256), lambda i: (i, 0, 0)),
-            pl.BlockSpec((step, 64, 2048), lambda i: (i, 0, 0)),
-            pl.BlockSpec((256, 2048), lambda i: (0, 0)),
-        ],
-        out_specs=pl.BlockSpec((1, step, 64, 2048), lambda i: (0, i, 0, 0)),
-        compiler_params=pltpu.CompilerParams(vmem_limit_bytes=32 * 2**20),
-        cost_estimate=pl.CostEstimate(flops=10**9, bytes_accessed=9 * 2**20, transcendentals=0),
-        name="map_gradient",
-    )(dy, lc, coli)
-    return grad, sg.reshape(2, 16, 2, 4, 128), sums[:, :16], sums[:, 16]
+    grad, sg, lg, bg = pl.pallas_call(
+        write_kernel,
+        out_shape=(
+            jax.ShapeDtypeStruct((1,) + big, BF16),
+            jax.ShapeDtypeStruct((32, 8, 128), F32),
+            jax.ShapeDtypeStruct((16, 16), F32),
+            jax.ShapeDtypeStruct((1, 16), F32),
+        ),
+        in_specs=[anywhere, vmem, vmem],
+        out_specs=(anywhere, vmem, vmem, vmem),
+        scratch_shapes=[dma(())],
+        compiler_params=pltpu.CompilerParams(vmem_limit_bytes=4 * 2**20),
+        cost_estimate=pl.CostEstimate(flops=0, bytes_accessed=8 * 2**20, transcendentals=0),
+        name="write_results",
+    )(fg, sg, sums)
+    return grad, sg.reshape(2, 16, 2, 4, 128), lg, bg.reshape(16)
 
 
 def solution(mesh):

time: 74.6 us -> 59.2 us (0.79)
  Pallas kernels: 68.6 us -> 58.3 us
  local copies, waits for them, and re-layouts: 5.18 us -> 0 us
    pallas_call x2, Pallas kernels: 68.6 us -> 58.3 us  [the longest x1 55.6 us: on_device(): pl.pallas_call(exchange_kernel, out_shape=(pltpu.VMEM(big, BF16), pltpu.V...]
    unnamed x12 -> x0, local copies, waits for them, and re-layouts: 4.49 us -> none
where the time goes in v1:
time: 59.2 us; the launch traced here: 59.1 us
  Pallas kernels  58.3 us (98%)
  between operations  0.8 us (1%)
    pallas_call x1, Pallas kernels, on_device(): pl.pallas_call(exchange_kernel, out_shape=(pltpu.VMEM(big, BF16), pltpu.V...  55.6 us
    pallas_call x1, Pallas kernels, on_device(): pl.pallas_call(write_kernel, out_shape=(jax.ShapeDtypeStruct((1,) + big,...  2.68 us

profile of v1, /device:TPU:1, one launch (start us, length us, event | category | flops | bytes accessed | tf_op | source)
XLA Modules:
  0.0 59.1 jit_solution(166315234571534258)
XLA Ops:
  0.6 55.6 %layer_exchange.1 = (bf16[16,64,2048]{2,1,0:T(8,128)(2,1)S(1)}, f32[32,8,128]{2,1,0:T(8,128)S(1)}, f32[16,128]{1,0:T(8,128)S(1)}) custom-call(bf16[16,64,2048]{2,1,0:T(8,128)(2,1)} %bitcast.6, bf16[16,64,2048]{2,1,0:T(8,128)(2,1)} %bitcast.7, bf16[2,1024,128]{2,1,0:T(8,128)(2,1)} %bitcast.8, bf16[16,16]{1,0:T(8,128)(2,1)} %lw_h.1, f32[1,16]{1,0:T(1,128)} %bitcast.10, ...), custom_call_target="tpu_custom_call" | custom-call | flops 8000000000 | bytes 16777216 | tf_op jit(solution)/shard_map/layer_exchange/pallas_call | solution.py:524
  56.2 2.7 %write_results.1 = (bf16[1,16,64,2048]{3,2,1,0:T(8,128)(2,1)}, f32[32,8,128]{2,1,0:T(8,128)}, f32[16,16]{1,0:T(8,128)}, f32[1,16]{1,0:T(1,128)}) custom-call(bf16[16,64,2048]{2,1,0:T(8,128)(2,1)S(1)} %get-tuple-element.11.fg, f32[32,8,128]{2,1,0:T(8,128)S(1)} %get-tuple-element.12.sg, f32[16,128]{1,0:T(8,128)S(1)} %get-tuple-element.13.sums), custom_call_target="tpu_custom_call" | custom-call | bytes 8388608 | tf_op jit(solution)/shard_map/write_results/pallas_call | solution.py:543

commit v2 on v1

--- a/solution.py
+++ b/solution.py
@@ -19,7 +19,7 @@
 CHIPS = SIDE * SIDE
 GROUPS = 4
 OFFSETS = (4, 0, 3, 5, 2, 6, 1, 7)
-STEP = 512
+STEP = 256
 PEERS = sorted(
     ((dy, dx) for dy in range(SIDE) for dx in range(SIDE) if dy or dx),
     key=lambda p: -(min(p[0], SIDE - p[0]) + min(p[1], SIDE - p[1])),
@@ -174,7 +174,9 @@
             snd[g, :, :, 16 * j : 16 * j + 16, :] = blk.reshape(2, CHIPS, 16, 128)
 
     def start_sibling(snd, sib, ss, rs, g):
-        to_sibling(snd.at[g, other], sib.at[g], ss.at[g], rs.at[g])
+        for half in range(2):
+            at = pl.ds(half * (CHIPS // 2), CHIPS // 2)
+            to_sibling(snd.at[g, other, at], sib.at[g, at], ss.at[g], rs.at[g])
 
     def pass_on(snd, sib, hb, rcv, rs, ds, dr, g):
         wait_for(sib.at[g], rs.at[g])
@@ -191,7 +193,9 @@
 
     def gather_forward(ga, arsem, fs, fr, g):
         wait_for(ga.at[g, core, pl.ds(0, CHIPS - 1)], arsem.at[g])
-        to_sibling(ga.at[g, core], ga.at[g, core], fs.at[g], fr.at[g])
+        for half in range(2):
+            at = pl.ds(half * (CHIPS // 2), CHIPS // 2)
+            to_sibling(ga.at[g, core, at], ga.at[g, core, at], fs.at[g], fr.at[g])
 
     def gather_end(ga, fr, g):
         wait_for(ga.at[g, other], fr.at[g])
@@ -246,6 +250,17 @@
 
     lax.fori_loop(0, 16, widen, 0)
 
+    lane = lax.broadcasted_iota(jnp.int32, (8, 128), 1)
+    double = jnp.where(lane == 0, 1.0, 2.0).astype(F32)
+
+    def mix(c, carry):
+        out_r, out_i = carry
+        wr, wi = wf[0, c], wf[1, c]
+        fr, fi = frd[c][None], fid[c][None]
+        return out_r + wr * fr - wi * fi, out_i + wr * fi + wi * fr
+
+    zero = jnp.zeros((8, 8, 128), F32)
+    mixed = (zero, zero)
     for g in range(GROUPS):
         total = arrived(rcv1, dr1, g)
         for c in range(4):
@@ -253,19 +268,9 @@
             imag = total[8 * c + 4 : 8 * c + 8]
             frd[4 * g + c] = jnp.concatenate([real, real], axis=0)
             fid[4 * g + c] = jnp.concatenate([imag, imag], axis=0)
-
-    lane = lax.broadcasted_iota(jnp.int32, (8, 128), 1)
-    double = jnp.where(lane == 0, 1.0, 2.0).astype(F32)
-
-    def mix(c, carry):
-        real, imag = carry
-        wr, wi = wf[0, c], wf[1, c]
-        fr, fi = frd[c][None], fid[c][None]
-        return real + wr * fr - wi * fi, imag + wr * fi + wi * fr
-
-    zero = jnp.zeros((8, 8, 128), F32)
-    real, imag = lax.fori_loop(0, 16, mix, (zero, zero))
-    gbuf[...] = (jnp.concatenate([real, imag], axis=1) * jnp.concatenate([double, double], axis=0)).astype(BF16)
+        mixed = lax.fori_loop(4 * g, 4 * g + 4, mix, mixed)
+    mixed_r, mixed_i = mixed
+    gbuf[...] = (jnp.concatenate([mixed_r, mixed_i], axis=1) * jnp.concatenate([double, double], axis=0)).astype(BF16)
 
     def pair_at(p):
         return lax.rem(z + OFFSETS[p], 8)
@@ -283,19 +288,25 @@
     dfr[...] = jnp.zeros_like(dfr)
     dfi[...] = jnp.zeros_like(dfi)
 
-    def gradient_arrived(g):
+    def input_terms(g):
         total = arrived(rcv2, dr2, g)
+        modes = []
         for j in range(2):
             q = pair_at(2 * g + j)
             a, b = total[16 * j : 16 * j + 8], total[16 * j + 8 : 16 * j + 16]
             gr = jnp.concatenate([a[:4], b[:4]], axis=0) * double
             gi = jnp.concatenate([a[4:], b[4:]], axis=0) * double
-            slot = 2 * g + j
             wr = wf[0, :, pl.ds(q, 1)].reshape(16, 8, 128)
             wi = wf[1, :, pl.ds(q, 1)].reshape(16, 8, 128)
-            fr, fi = frd[...], fid[...]
             dfr[...] += wr * gr[None] + wi * gi[None]
             dfi[...] += wr * gi[None] - wi * gr[None]
+            modes.append((gr, gi))
+        return modes
+
+    def weight_terms(g, modes):
+        for j, (gr, gi) in enumerate(modes):
+            slot = 2 * g + j
+            fr, fi = frd[...], fid[...]
             term = jnp.concatenate(
                 [
                     (gr[None] * fr + gi[None] * fi).reshape(128, 128),
@@ -309,8 +320,11 @@
                 dwsnd[slot] = term
                 pltpu.make_async_remote_copy(
                     src_ref=dwsnd.at[slot], dst_ref=dwrcv.at[z], send_sem=dws.at[slot],
-                    recv_sem=dwr, device_id={"dp": q}, device_id_type=MESH,
+                    recv_sem=dwr, device_id={"dp": pair_at(slot)}, device_id_type=MESH,
                 ).start()
+
+    def gradient_arrived(g):
+        weight_terms(g, input_terms(g))
 
     for g in range(GROUPS):
         gather_end(ga1, fr1, g)
@@ -329,12 +343,13 @@
                 grads.append(grad)
             return acc + dot(jnp.concatenate(grads, axis=0), colf[at, :])
 
-        acc = chunk(1, chunk(0, jnp.zeros((256, 256), F32)))
-        if g > 0:
-            pass_on(snd2, sib2, hb2, rcv2, rs2, ds2, dr2, g - 1)
         if g + 1 < GROUPS:
             gather_forward(ga1, ar1, fs1, fr1, g + 1)
-        acc = chunk(3, chunk(2, acc))
+        acc = jnp.zeros((256, 256), F32)
+        for w in range(2048 // STEP):
+            if g > 0 and w == 6:
+                pass_on(snd2, sib2, hb2, rcv2, rs2, ds2, dr2, g - 1)
+            acc = chunk(w, acc)
         for j in range(2):
             for o in range(2):
                 at = 128 * j + 64 * o
@@ -360,8 +375,8 @@
             fg_o[:, at, w : w + STEP] = part.astype(BF16).reshape(16, 16, STEP)
 
     lacc[...] = outer_block(0)
+    gradient_arrived(0)
     pass_on(snd2, sib2, hb2, rcv2, rs2, ds2, dr2, GROUPS - 1)
-    gradient_arrived(0)
     lacc[...] += outer_block(1)
     gradient_arrived(1)
     lacc[...] += outer_block(2)
@@ -389,7 +404,7 @@
     back_block(2)
     back_block(3)
 
-    gradient_arrived(GROUPS - 1)
+    last = input_terms(GROUPS - 1)
 
     for g in range(GROUPS):
         for j in range(2):
@@ -401,6 +416,7 @@
                     parts.append(both[:4] + both[4:])
             ga2[g, core, chip, 16 * j : 16 * j + 16, :] = jnp.concatenate(parts, axis=0).astype(BF16)
         gather_start(ga2, as2, ar2, g)
+    weight_terms(GROUPS - 1, last)
 
     wait_for(payrow.at[pl.ds(0, CHIPS - 1)], pr.at[1])
     pay[2] = jnp.sum(payrow[...], axis=0)

time: 59.2 us -> 57.5 us (0.971)
  Pallas kernels: 58.3 us -> 56.6 us
    pallas_call x1, Pallas kernels: 55.6 us -> 53.9 us  [on_device(): pl.pallas_call(exchange_kernel, out_shape=(pltpu.VMEM(big, BF16), pltpu.V...]
where the time goes in v2:
time: 57.5 us; the launch traced here: 57.4 us
  Pallas kernels  56.6 us (98%)
  between operations  0.8 us (1%)
    pallas_call x1, Pallas kernels, on_device(): pl.pallas_call(exchange_kernel, out_shape=(pltpu.VMEM(big, BF16), pltpu.V...  53.9 us
    pallas_call x1, Pallas kernels, on_device(): pl.pallas_call(write_kernel, out_shape=(jax.ShapeDtypeStruct((1,) + big,...  2.68 us

profile of v2, /device:TPU:1, one launch (start us, length us, event | category | flops | bytes accessed | tf_op | source)
XLA Modules:
  0.0 57.4 jit_solution(11958127324678226714)
XLA Ops:
  0.6 53.9 %layer_exchange.1 = (bf16[16,64,2048]{2,1,0:T(8,128)(2,1)S(1)}, f32[32,8,128]{2,1,0:T(8,128)S(1)}, f32[16,128]{1,0:T(8,128)S(1)}) custom-call(bf16[16,64,2048]{2,1,0:T(8,128)(2,1)} %bitcast.6, bf16[16,64,2048]{2,1,0:T(8,128)(2,1)} %bitcast.7, bf16[2,1024,128]{2,1,0:T(8,128)(2,1)} %bitcast.8, bf16[16,16]{1,0:T(8,128)(2,1)} %lw_h.1, f32[1,16]{1,0:T(1,128)} %bitcast.10, ...), custom_call_target="tpu_custom_call" | custom-call | flops 8000000000 | bytes 16777216 | tf_op jit(solution)/shard_map/layer_exchange/pallas_call | solution.py:540
  54.6 2.7 %write_results.1 = (bf16[1,16,64,2048]{3,2,1,0:T(8,128)(2,1)}, f32[32,8,128]{2,1,0:T(8,128)}, f32[16,16]{1,0:T(8,128)}, f32[1,16]{1,0:T(1,128)}) custom-call(bf16[16,64,2048]{2,1,0:T(8,128)(2,1)S(1)} %get-tuple-element.11.fg, f32[32,8,128]{2,1,0:T(8,128)S(1)} %get-tuple-element.12.sg, f32[16,128]{1,0:T(8,128)S(1)} %get-tuple-element.13.sums), custom_call_target="tpu_custom_call" | custom-call | bytes 8388608 | tf_op jit(solution)/shard_map/write_results/pallas_call | solution.py:559

commit v3 on v2

--- a/solution.py
+++ b/solution.py
@@ -431,6 +431,22 @@
     for g in range(GROUPS):
         if g + 1 < GROUPS:
             gather_forward(ga2, ar2, fs2, fr2, g + 1)
+        if g == GROUPS - 1:
+            wait_for(dwrcv.at[pl.ds(0, 7)], dwr)
+            total = dwrcv[0].astype(F32)
+            for k in range(1, 8):
+                total = total + dwrcv[k].astype(F32)
+            sg_o[...] = total.reshape(32, 8, 128)
+            for k in range(GROUPS):
+                wait_for(snd1.at[k, 0], ss1.at[k])
+                wait_for(hb1.at[k, pl.ds(0, CHIPS - 1)], ds1.at[k])
+                wait_for(snd2.at[k, 0], ss2.at[k])
+                wait_for(hb2.at[k, pl.ds(0, CHIPS - 1)], ds2.at[k])
+                wait_for(ga1.at[k, core, pl.ds(0, CHIPS - 1)], as1.at[k])
+                wait_for(ga1.at[k, core], fs1.at[k])
+            for slot in range(8):
+                if OFFSETS[slot] != 0:
+                    wait_for(dwsnd.at[slot], dws.at[slot])
         gather_end(ga2, fr2, g)
         ybuf[...] = row_inverse(ga2, g)
         for w in range(0, 2048, STEP):
@@ -440,28 +456,13 @@
                 (spectral + local_part).astype(BF16).reshape(4, 64, STEP)
             )
 
-    wait_for(dwrcv.at[pl.ds(0, 7)], dwr)
-    total = dwrcv[0].astype(F32)
-    for k in range(1, 8):
-        total = total + dwrcv[k].astype(F32)
-    sg_o[...] = total.reshape(32, 8, 128)
-
     wait_for(paydp.at[pl.ds(0, 7)], pr.at[2])
     scale = 1.0 / math.sqrt(8 * 2048 * 2048)
     sums_o[...] = scale * jnp.sum(paydp[...], axis=0)
 
     for g in range(GROUPS):
-        wait_for(snd1.at[g, 0], ss1.at[g])
-        wait_for(hb1.at[g, pl.ds(0, CHIPS - 1)], ds1.at[g])
-        wait_for(snd2.at[g, 0], ss2.at[g])
-        wait_for(hb2.at[g, pl.ds(0, CHIPS - 1)], ds2.at[g])
-        wait_for(ga1.at[g, core, pl.ds(0, CHIPS - 1)], as1.at[g])
-        wait_for(ga1.at[g, core], fs1.at[g])
         wait_for(ga2.at[g, core, pl.ds(0, CHIPS - 1)], as2.at[g])
         wait_for(ga2.at[g, core], fs2.at[g])
-    for slot in range(8):
-        if OFFSETS[slot] != 0:
-            wait_for(dwsnd.at[slot], dws.at[slot])
     wait_for(pay.at[0], ps.at[0])
     wait_for(payrow.at[pl.ds(0, CHIPS - 1)], ps.at[1])
     wait_for(paydp.at[pl.ds(0, 7)], ps.at[2])

time: 57.5 us -> 57.5 us (level)
  no operation moved by 1% of the time
where the time goes in v3:
time: 57.5 us; the launch traced here: 57.4 us
  Pallas kernels  56.6 us (98%)
  between operations  0.8 us (1%)
    pallas_call x1, Pallas kernels, on_device(): pl.pallas_call(exchange_kernel, out_shape=(pltpu.VMEM(big, BF16), pltpu.V...  53.9 us
    pallas_call x1, Pallas kernels, on_device(): pl.pallas_call(write_kernel, out_shape=(jax.ShapeDtypeStruct((1,) + big,...  2.68 us

profile of v3, /device:TPU:1, one launch (start us, length us, event | category | flops | bytes accessed | tf_op | source)
XLA Modules:
  0.0 57.4 jit_solution(13588402684772504914)
XLA Ops:
  0.6 53.9 %layer_exchange.1 = (bf16[16,64,2048]{2,1,0:T(8,128)(2,1)S(1)}, f32[32,8,128]{2,1,0:T(8,128)S(1)}, f32[16,128]{1,0:T(8,128)S(1)}) custom-call(bf16[16,64,2048]{2,1,0:T(8,128)(2,1)} %bitcast.6, bf16[16,64,2048]{2,1,0:T(8,128)(2,1)} %bitcast.7, bf16[2,1024,128]{2,1,0:T(8,128)(2,1)} %bitcast.8, bf16[16,16]{1,0:T(8,128)(2,1)} %lw_h.1, f32[1,16]{1,0:T(1,128)} %bitcast.10, ...), custom_call_target="tpu_custom_call" | custom-call | flops 8000000000 | bytes 16777216 | tf_op jit(solution)/shard_map/layer_exchange/pallas_call | solution.py:541
  54.5 2.7 %write_results.1 = (bf16[1,16,64,2048]{3,2,1,0:T(8,128)(2,1)}, f32[32,8,128]{2,1,0:T(8,128)}, f32[16,16]{1,0:T(8,128)}, f32[1,16]{1,0:T(1,128)}) custom-call(bf16[16,64,2048]{2,1,0:T(8,128)(2,1)S(1)} %get-tuple-element.11.fg, f32[32,8,128]{2,1,0:T(8,128)S(1)} %get-tuple-element.12.sg, f32[16,128]{1,0:T(8,128)S(1)} %get-tuple-element.13.sums), custom_call_target="tpu_custom_call" | custom-call | bytes 8388608 | tf_op jit(solution)/shard_map/write_results/pallas_call | solution.py:560
